TPU v7x, 32 devices: a whole 2x2x4 slice. The times are simulated.
32 devices in a mesh: rows: 4 (over y, core), chan: 8 (over z, x).
Axes of the slice: x: 2, y: 2, z: 4, core: 2. Of those that a mesh axis runs over, the one named last changes fastest.
Arguments:
- features: bfloat16 [256, 1536, 256], P('rows', 'chan'), may hold values from -6 to 6
- mixing: float32 [3, 256, 256], P(None, 'rows'), may hold values from 0 to 1, as said below
- decay_rate: float32 [256, 256], P('rows'), may hold values from 0 to 0.5, as said below
- gate_input: bfloat16 [256, 1536, 256], P('rows', 'chan'), may hold values from -6 to 6
- out_weight: bfloat16 [1536, 1536], replicated, may hold values from -0.15625 to 0.15625
Outputs:
- projected: bfloat16 [256, 1536, 256], P(('rows', 'chan'))
Inputs may be any that keep to these rules, and one draw needn't show every extreme that they name: `mixing`: at every row and column the three weights are positive where their neighbour exists, the left weight is zero at column 0 and the right weight at column 255, and the three sum to one. `decay_rate`: every entry is positive.
All inputs are finite; a program needn't handle non-finite values.
Results may differ from a plain program's by a relative error of at most 0.0049.
Values may be sent and summed in bfloat16 or wider, within the bound.
A program may use at most 128 MiB of HBM per device.

v0:
```python
import jax
import jax.numpy as jnp
from jax import lax
from jax.sharding import PartitionSpec as P

BLOCK = 16


def from_behind(value, axis, by):
    peers = lax.axis_size(axis)
    pairs = [(i, i + by) for i in range(peers) if 0 <= i + by < peers]
    return lax.ppermute(value, axis, pairs)


def spread(current, left_w, mid_w, right_w):
    edge_col = jnp.zeros(current.shape[:-1] + (1,), current.dtype)
    before_col = jnp.concatenate([edge_col, current[..., :-1]], axis=-1)
    after_col = jnp.concatenate([current[..., 1:], edge_col], axis=-1)
    return left_w * before_col + mid_w * current + right_w * after_col


def shards(features, mixing, decay_rate, gate_input, out_weight):
    rows_here, channels, col_count = features.shape
    blocks = rows_here // BLOCK
    highest = lax.Precision.HIGHEST
    retain = 1.0 - decay_rate
    weights = retain[None] * mixing
    in_scale = jnp.sqrt(decay_rate)
    forcing = in_scale[:, None, :] * features.astype(jnp.float32)
    coef_steps = weights.reshape(3, blocks, BLOCK, col_count).transpose(2, 0, 1, 3)
    force_steps = forcing.reshape(blocks, BLOCK, channels, col_count).swapaxes(0, 1)
    identity_op = jnp.eye(col_count, dtype=jnp.float32)

    def advance(carry_pair, inputs):
        local_st, op_stack = carry_pair
        coef_row, push_row = inputs
        left_w = coef_row[0][:, None, :]
        mid_w = coef_row[1][:, None, :]
        right_w = coef_row[2][:, None, :]
        local_st = spread(local_st, left_w, mid_w, right_w) + push_row
        op_stack = spread(op_stack, left_w, mid_w, right_w)
        return ((local_st, op_stack), (local_st, op_stack))

    initial = (
        jnp.zeros((blocks, channels, col_count), jnp.float32),
        jnp.broadcast_to(identity_op, (blocks, col_count, col_count)),
    )
    _, (local_all, ops_all) = lax.scan(advance, initial, (coef_steps, force_steps))
    last_ops = ops_all[-1]
    last_local = local_all[-1]

    def carry_on(current, inputs):
        block_op, loc_end = inputs
        return (jnp.dot(current, block_op, precision=highest) + loc_end, current)

    def compose_ops(running, block_op):
        return (jnp.dot(running, block_op, precision=highest), running)

    summary, _ = lax.scan(compose_ops, identity_op, last_ops)
    zero_state = jnp.zeros((channels, col_count), jnp.float32)
    offset, _ = lax.scan(carry_on, zero_state, (last_ops, last_local))

    def relay_step(turn_index, current):
        return from_behind(jnp.dot(current, summary, precision=highest) + offset, "rows", 1)

    incoming = lax.fori_loop(0, lax.axis_size("rows") - 1, relay_step, zero_state)
    _, starts = lax.scan(carry_on, incoming, (last_ops, last_local))
    states = local_all + jnp.einsum("bcv,jbvw->jbcw", starts, ops_all, precision=highest)
    states = states.swapaxes(0, 1).reshape(rows_here, channels, col_count)
    mixed_in = (states * jax.nn.silu(gate_input.astype(jnp.float32))).astype(jnp.bfloat16)
    return jnp.einsum(
        "oc,rcw->row",
        out_weight,
        lax.all_to_all(mixed_in, "chan", split_axis=0, concat_axis=1, tiled=True),
        preferred_element_type=jnp.float32,
    ).astype(jnp.bfloat16)


def solution(mesh):
    in_specs = (
        P("rows", "chan", None),
        P(None, "rows", None),
        P("rows", None),
        P("rows", "chan", None),
        P(),
    )
    out_specs = P(("rows", "chan"), None, None)
    return jax.shard_map(shards, mesh=mesh, in_specs=in_specs, out_specs=out_specs, check_vma=False)
```

profile of v0, /device:TPU:5, one launch (start us, length us, event | category | flops | bytes accessed | tf_op | source)
XLA Modules:
  0.0 313.3 jit_solution(9483328686287651081)
XLA Ops:
  1.1 9.2 %convert_multiply_fusion.1 = f32[64,192,256]{2,1,0:T(8,128)} fusion(bf16[64,192,256]{2,1,0:T(8,128)(2,1)} %param.15, f32[64,256]{1,0:T(8,128)S(1)} %get-tuple-element.261), kind=kLoop, calls=%fused_computation.40 | loop fusion | flops 6291456 | bytes 18939904 | tf_op jit(solution)/shard_map/mul | solution.py:29
  10.4 82.1 %while.63 = (s32[]{:T(128)}, f32[4,192,256]{2,1,0:T(8,128)S(1)}, f32[4,256,256]{2,1,0:T(8,128)S(1)}, f32[16,4,192,256]{3,2,1,0:T(8,128)}, f32[16,4,256,256]{3,2,...) while((s32[]{:T(128)}, f32[4,192,256]{2,1,0:T(8,128)S(1)}, ...), condition=%wide.region_1.2_spmd.clone, body=%wide.region_0.1_spmd.clone.sunk | while | flops 2883589 | bytes 18906268 | solution.py:48
  12.9 2.7 bitcast_dynamic-update-slice_fusion.7
  18.0 2.7 bitcast_dynamic-update-slice_fusion.7
  23.1 2.7 bitcast_dynamic-update-slice_fusion.7
  28.3 2.7 bitcast_dynamic-update-slice_fusion.7
  33.4 2.7 bitcast_dynamic-update-slice_fusion.7
  36.5 1.7 bitcast_dynamic-update-slice_fusion.8
  38.5 2.7 bitcast_dynamic-update-slice_fusion.7
  43.6 2.7 bitcast_dynamic-update-slice_fusion.7
  46.7 1.7 bitcast_dynamic-update-slice_fusion.8
  48.8 2.7 bitcast_dynamic-update-slice_fusion.7
  51.9 1.7 bitcast_dynamic-update-slice_fusion.8
  54.0 2.7 bitcast_dynamic-update-slice_fusion.7
  59.1 2.7 bitcast_dynamic-update-slice_fusion.7
  64.2 2.7 bitcast_dynamic-update-slice_fusion.7
  69.3 2.7 bitcast_dynamic-update-slice_fusion.7
  72.4 1.7 bitcast_dynamic-update-slice_fusion.8
  74.5 2.7 bitcast_dynamic-update-slice_fusion.7
  79.5 2.7 bitcast_dynamic-update-slice_fusion.7
  84.7 2.7 bitcast_dynamic-update-slice_fusion.7
  89.8 2.7 bitcast_dynamic-update-slice_fusion.7
  96.6 2.6 while.60
  99.3 18.5 %while.61 = (s32[]{:T(128)}, f32[192,256]{1,0:T(8,128)S(1)}, f32[256,256]{1,0:T(8,128)S(1)}, f32[192,256]{1,0:T(8,128)S(1)}, s32[]{:T(128)}) while((s32[]{:T(128)}, f32[192,256]{1,0:T(8,128)S(1)}, f32[256,256]{1,0:T(8,128)S(1)}, f32[192,256]{1,0:T(8,128)S(1)}, s32[]{:T(128)}) %tuple.112), condition=%wide.region_7.8_spmd, body=%wide.region_6.7_spmd.sunk | while | flops 151044096 | bytes 1638501 | solution.py:66
  101.0 2.2 collective-permute-done
  104.8 5.7 %collective-permute-done = f32[192,256]{1,0:T(8,128)S(1)} collective-permute-done((f32[192,256]{1,0:T(8,128)S(1)}, f32[192,256]{1,0:T(8,128)S(1)}, u32[]{:S(2)}, u32[]{:S(2)}) %collective-permute-start) | collective-permute-done | bytes 196640 | tf_op jit(solution)/shard_map/while/body/eval_jaxpr/ppermute | solution.py:12
  112.2 5.7 %collective-permute-done = f32[192,256]{1,0:T(8,128)S(1)} collective-permute-done((f32[192,256]{1,0:T(8,128)S(1)}, f32[192,256]{1,0:T(8,128)S(1)}, u32[]{:S(2)}, u32[]{:S(2)}) %collective-permute-start) | collective-permute-done | bytes 196640 | tf_op jit(solution)/shard_map/while/body/eval_jaxpr/ppermute | solution.py:12
  119.5 21.2 %bitcast_add_fusion.1 = f32[16,4,192,256]{3,2,0,1:T(8,128)} fusion(f32[16,4,192,256]{3,2,1,0:T(8,128)} %get-tuple-element.131, f32[16,4,256,256]{3,2,1,0:T(8,128)} %get-tuple-element.132, f32[4,192,256]{2,1,0:T(8,128)S(1)} %get-tuple-element.136), kind=kOutput, calls=%fused_computation.39 | convolution fusion | flops 9666822144 | bytes 42729472 | tf_op jit(solution)/shard_map/bcv,jbvw->jbcw/dot_general | solution.py:68
  140.7 8.6 %fusion.21 = bf16[64,192,256]{2,1,0:T(8,128)(2,1)S(1)} fusion(bf16[64,192,256]{2,1,0:T(8,128)(2,1)} %param.18, f32[16,4,192,256]{3,2,0,1:T(8,128)} %bitcast_add_fusion.1), kind=kLoop, calls=%fused_computation.41 | loop fusion | flops 22020096 | bytes 25165824 | tf_op jit(solution)/shard_map/convert_element_type | solution.py:70
  149.4 141.9 %all_to_all.18 = bf16[64,192,256]{2,1,0:T(8,128)(2,1)S(1)} all-to-all(bf16[64,192,256]{2,1,0:T(8,128)(2,1)S(1)} %fusion.21), channel_id=1, replica_groups=mesh['rows'=4,'chan'=8] {'chan'}, dimensions={0} | all-to-all | bytes 12582912 | tf_op jit(solution)/shard_map/all_to_all | solution.py:74
  292.4 12.4 %convert_bitcast_fusion = bf16[8,1536,256]{1,2,0:T(8,128)(2,1)} fusion(bf16[8,1536,256]{2,1,0:T(8,128)(2,1)S(1)} %bitcast.114, bf16[1536,1536]{1,0:T(8,128)(2,1)S(1)} %bitcast.119), kind=kOutput, calls=%fused_computation.42 | convolution fusion | flops 9666822144 | bytes 17301504 | tf_op jit(solution)/shard_map/oc,rcw->row/dot_general | solution.py:71
  304.7 8.6 %copy.28 = bf16[8,1536,256]{2,1,0:T(8,128)(2,1)} copy(bf16[8,1536,256]{1,2,0:T(8,128)(2,1)} %convert_bitcast_fusion) | data formatting | bytes 12582912 | tf_op jit(solution)/shard_map/convert_element_type | solution.py:76
  (166 shorter events, 49.9 us)
Async XLA Ops:
  0.0 10.3 %copy-start = (f32[3,64,256]{2,1,0:T(8,128)S(1)}, f32[3,64,256]{2,1,0:T(8,128)}, u32[]{:S(2)}) copy-start(f32[3,64,256]{2,1,0:T(8,128)} %param.16) | copy-start | bytes 589828
  99.7 3.5 %collective-permute-start = (f32[192,256]{1,0:T(8,128)S(1)}, f32[192,256]{1,0:T(8,128)S(1)}, u32[]{:S(2)}, u32[]{:S(2)}) collective-permute-start(f32[192,256]{1,0:T(8,128)S(1)} %convolution_add_fusion.2), channel_id=1, source_target_pairs={{0,8},{8,16},{16,24},{1,9},{9,17},{17,25},{2,10},{10,18},{18,26},{... | collective-permute-start | bytes 589832 | tf_op jit(solution)/shard_map/while/body/eval_jaxpr/ppermute | solution.py:12
  103.5 7.0 %collective-permute-start = (f32[192,256]{1,0:T(8,128)S(1)}, f32[192,256]{1,0:T(8,128)S(1)}, u32[]{:S(2)}, u32[]{:S(2)}) collective-permute-start(f32[192,256]{1,0:T(8,128)S(1)} %convolution_add_fusion.2), channel_id=1, source_target_pairs={{0,8},{8,16},{16,24},{1,9},{9,17},{17,25},{2,10},{10,18},{18,26},{... | collective-permute-start | bytes 589832 | tf_op jit(solution)/shard_map/while/body/eval_jaxpr/ppermute | solution.py:12
  110.9 7.0 %collective-permute-start = (f32[192,256]{1,0:T(8,128)S(1)}, f32[192,256]{1,0:T(8,128)S(1)}, u32[]{:S(2)}, u32[]{:S(2)}) collective-permute-start(f32[192,256]{1,0:T(8,128)S(1)} %convolution_add_fusion.2), channel_id=1, source_target_pairs={{0,8},{8,16},{16,24},{1,9},{9,17},{17,25},{2,10},{10,18},{18,26},{... | collective-permute-start | bytes 589832 | tf_op jit(solution)/shard_map/while/body/eval_jaxpr/ppermute | solution.py:12
  149.4 142.7 %slice-start = ((s8[4718592]{0:T(1024)(128)(4,1)}), s8[4194304]{0:T(1024)(128)(4,1)S(1)}, s32[]{:S(2)}) async-start(s8[4718592]{0:T(1024)(128)(4,1)} %bitcast.118), calls=%async_computation.1 | async-start | bytes 8388608
  291.3 1.0 slice-start.1
where the time goes:
time: 317 us; the launch traced here: 313 us
  blocking collectives  142 us (45%)
  other arithmetic  89.9 us (28%)
  matrix products  39.7 us (13%)
  local copies, waits for them, and re-layouts  23.2 us (7%)
  waiting for transfers between devices  13.6 us (4%)
  starting transfers between devices  3.88 us (1%)
    all_to_all x1, blocking collectives, shards(): lax.all_to_all(mixed_in, 'chan', split_axis=0, concat_axis=1, tiled=True)  142 us
    dynamic_update_slice x32, other arithmetic, shards(): lax.scan(advance, initial, (coef_steps, force_steps))  70 us
    dot_general x1, matrix products, shards(): jnp.einsum('bcv,jbvw->jbcw', starts, ops_all, precision=highest)  21.2 us
    ppermute x3, waiting for transfers between devices, from_behind(): return lax.ppermute(value, axis, pairs)  13.6 us
    dot_general x1, matrix products, shards(): jnp.einsum('oc,rcw->row', out_weight, lax.all_to_all(mixed_in, 'chan', sp...  12.4 us
    slice x32, local copies, waits for them, and re-layouts, spread(): before_col = jnp.concatenate([edge_col, current[..., :-1]], axis=-1)  10.1 us
    mul x1, other arithmetic, shards(): forcing = in_scale[:, None, :] * features.astype(jnp.float32)  9.2 us
    convert_element_type x1, other arithmetic, shards(): (states * jax.nn.silu(gate_input.astype(jnp.float32))).astype(jnp.bfloat16)  8.64 us
  transfers between devices with their start and end apart: 3, of which 3 were waited for; matrix products, arithmetic and copies ran while one was open for 0% of the time, Pallas kernels for 0%

commit v1 on v0

v1 whole, which is shorter than its diff:
```python
import functools

import jax
import jax.numpy as jnp
from jax import lax
from jax.experimental import pallas as pl
from jax.experimental.pallas import tpu as pltpu
from jax.sharding import PartitionSpec as P

MESH = pl.DeviceIdType.MESH
HIGHEST = lax.Precision.HIGHEST


def tile_of(size, choices):
    return next(t for t in choices if size % t == 0)


def partner(me, k, n):
    half = n // 2
    side, place = me // half, me % half
    across = (1 - side) * half + (place + k) % half
    beside = side * half + (place + 1 + k - half) % half
    return jnp.where(k < half, across, beside)


def kernel(n_rows, n, feat_hbm, mix_ref, decay_ref, gate_hbm, w_hbm, out_hbm,
           feat, gate, weight, coef, scale, band, ops, starts, tail, incoming, outgoing, sent, got, result,
           feat_sem, gate_sem, weight_sem, out_sem, send_sem, recv_sem, relay_send, relay_recv):
    _, chunk, ch, cols = feat.shape
    c_out = weight.shape[0]
    p, me = lax.axis_index("rows"), lax.axis_index("chan")
    tile = tile_of(ch, (64, 48, 32, 16))
    tiles = ch // tile
    o_tile = tile_of(c_out, (256, 128, 64, 32, 16))

    def feat_copy(j):
        return pltpu.make_async_copy(feat_hbm.at[j], feat.at[j], feat_sem.at[j])

    def gate_copy(j):
        return pltpu.make_async_copy(gate_hbm.at[j], gate.at[j], gate_sem.at[j])

    weight_copy = pltpu.make_async_copy(w_hbm, weight, weight_sem)

    @pl.loop(0, n)
    def _(j):
        feat_copy(j).start()

    @pl.loop(0, n)
    def _(j):
        gate_copy(j).start()

    weight_copy.start()

    barrier = pltpu.get_barrier_semaphore()

    @pl.loop(0, n - 1)
    def _(k):
        pl.semaphore_signal(barrier, inc=1, device_id={"chan": partner(me, k, n)}, device_id_type=MESH)

    @pl.when(p > 0)
    def _():
        pl.semaphore_signal(barrier, inc=1, device_id={"rows": p - 1}, device_id_type=MESH)

    @pl.when(p < n_rows - 1)
    def _():
        pl.semaphore_signal(barrier, inc=1, device_id={"rows": p + 1}, device_id_type=MESH)

    retain = 1.0 - decay_ref[...]
    for s in range(3):
        coef[s] = retain * mix_ref[s]
    scale[...] = jnp.sqrt(decay_ref[...])

    def step(state, j, row):
        left_w = coef[0, j, pl.ds(row, 1), :]
        mid_w = coef[1, j, pl.ds(row, 1), :]
        right_w = coef[2, j, pl.ds(row, 1), :]
        return left_w * pltpu.roll(state, 1, 1) + mid_w * state + right_w * pltpu.roll(state, cols - 1, 1)

    def advance(state, j, row, at):
        push = scale[j, pl.ds(row, 1), :] * feat[j, row, at, :].astype(jnp.float32)
        return step(state, j, row) + push

    tail[...] = jnp.zeros_like(tail)

    @pl.loop(0, n)
    def _(j):
        feat_copy(j).wait()

        @pl.loop(0, tiles)
        def _(t):
            at = pl.ds(pl.multiple_of(t * tile, tile), tile)
            state = tail[at, :]
            starts[j, at, :] = state
            for row in range(chunk):
                state = advance(state, j, row, at)
            tail[at, :] = state

    @pl.when(p > 0)
    def _():
        depth = band.shape[1]
        diagonal = lax.broadcasted_iota(jnp.int32, band.shape, 1)
        value = jnp.where(diagonal == chunk, 1.0, 0.0).astype(jnp.float32)
        for row in range(chunk):
            below = pltpu.roll(pltpu.roll(value, depth - 1, 1), 1, 2)
            above = pltpu.roll(pltpu.roll(value, 1, 1), cols - 1, 2)
            value = (coef[0, :, row:row + 1, :] * below + coef[1, :, row:row + 1, :] * value
                     + coef[2, :, row:row + 1, :] * above)
        band[...] = value
        offset = (lax.broadcasted_iota(jnp.int32, (cols, cols), 0)
                  - lax.broadcasted_iota(jnp.int32, (cols, cols), 1))
        ops[0] = jnp.where(offset == 0, 1.0, 0.0).astype(jnp.float32)

        @pl.loop(0, n)
        def _(j):
            dense = jnp.zeros((cols, cols), jnp.float32)
            for k in range(2 * chunk + 1):
                dense = jnp.where(offset == k - chunk, band[j, k:k + 1, :], dense)
            ops[j + 1] = jnp.dot(ops[j], dense, precision=HIGHEST, preferred_element_type=jnp.float32)

    pl.semaphore_wait(barrier, n - 1 + jnp.where(p > 0, 1, 0) + jnp.where(p < n_rows - 1, 1, 0))

    def relay(device):
        return pltpu.make_async_remote_copy(
            src_ref=outgoing, dst_ref=incoming, send_sem=relay_send, recv_sem=relay_recv,
            device_id={"rows": device}, device_id_type=MESH)

    @pl.when(p > 0)
    def _():
        relay(p - 1).wait_recv()

    @pl.when(p < n_rows - 1)
    def _():
        @pl.when(p == 0)
        def _():
            outgoing[...] = tail[...]

        @pl.when(p > 0)
        def _():
            outgoing[...] = tail[...] + jnp.dot(
                incoming[...], ops[n], precision=HIGHEST, preferred_element_type=jnp.float32)

        relay(p + 1).start()

    def send(row, k):
        return pltpu.make_async_remote_copy(
            src_ref=sent.at[k, row], dst_ref=got.at[row, pl.ds(pl.multiple_of(me * ch, ch), ch), :],
            send_sem=send_sem.at[row, k], recv_sem=recv_sem.at[row, k],
            device_id={"chan": partner(me, k, n)}, device_id_type=MESH)

    def gated_row(j, row, put):
        @pl.loop(0, tiles)
        def _(t):
            at = pl.ds(pl.multiple_of(t * tile, tile), tile)
            state = advance(starts[j, at, :], j, row, at)
            starts[j, at, :] = state
            v = gate[j, row, at, :].astype(jnp.float32)
            put(t, (state * (v / (1.0 + jnp.exp(-v)))).astype(jnp.bfloat16))

    @pl.loop(0, chunk)
    def _(row):
        @pl.loop(0, n)
        def _(k):
            j = partner(me, k, n)

            @pl.when(row == 0)
            def _():
                gate_copy(j).wait()

                @pl.when(p > 0)
                def _():
                    starts[j] = starts[j] + jnp.dot(
                        incoming[...], ops[j], precision=HIGHEST, preferred_element_type=jnp.float32)

            @pl.when(k < n - 1)
            def _():
                def put(t, value):
                    sent[k, row, pl.ds(pl.multiple_of(t * tile, tile), tile), :] = value

                gated_row(j, row, put)
                send(row, k).start()

            @pl.when(k == n - 1)
            def _():
                def put(t, value):
                    got[row, pl.ds(pl.multiple_of(me * ch + t * tile, tile), tile), :] = value

                gated_row(j, row, put)

    weight_copy.wait()

    def out_copy(row):
        return pltpu.make_async_copy(result.at[row], out_hbm.at[row], out_sem.at[row])

    @pl.loop(0, chunk)
    def _(row):
        @pl.loop(0, n - 1)
        def _(k):
            send(row, k).wait_recv()

        @pl.loop(0, c_out // o_tile)
        def _(o):
            at = pl.ds(pl.multiple_of(o * o_tile, o_tile), o_tile)
            result[row, at, :] = jnp.dot(
                weight[at, :], got[row], preferred_element_type=jnp.float32).astype(jnp.bfloat16)

        out_copy(row).start()

    @pl.loop(0, chunk)
    def _(row):
        @pl.loop(0, n - 1)
        def _(k):
            send(row, k).wait_send()

        out_copy(row).wait()

    @pl.when(p < n_rows - 1)
    def _():
        relay(p + 1).wait_send()


def shards(n_rows, n, features, mixing, decay_rate, gate_input, out_weight):
    rows_here, ch, cols = features.shape
    chunk = rows_here // n
    c_out, c_in = out_weight.shape
    depth = -(-(2 * chunk + 1) // 8) * 8
    f32, bf16 = jnp.float32, jnp.bfloat16
    any_spec = pl.BlockSpec(memory_space=pl.ANY)
    vmem_spec = pl.BlockSpec(memory_space=pltpu.VMEM)
    dma = pltpu.SemaphoreType.DMA
    flops = 2 * chunk * c_out * c_in * cols
    return pl.pallas_call(
        functools.partial(kernel, n_rows, n),
        out_shape=jax.ShapeDtypeStruct((chunk, c_out, cols), bf16),
        in_specs=[any_spec, vmem_spec, vmem_spec, any_spec, any_spec],
        out_specs=any_spec,
        scratch_shapes=[
            pltpu.VMEM((n, chunk, ch, cols), bf16),
            pltpu.VMEM((n, chunk, ch, cols), bf16),
            pltpu.VMEM((c_out, c_in), bf16),
            pltpu.VMEM((3, n, chunk, cols), f32),
            pltpu.VMEM((n, chunk, cols), f32),
            pltpu.VMEM((n, depth, cols), f32),
            pltpu.VMEM((n + 1, cols, cols), f32),
            pltpu.VMEM((n, ch, cols), f32),
            pltpu.VMEM((ch, cols), f32),
            pltpu.VMEM((ch, cols), f32),
            pltpu.VMEM((ch, cols), f32),
            pltpu.VMEM((n, chunk, ch, cols), bf16),
            pltpu.VMEM((chunk, c_in, cols), bf16),
            pltpu.VMEM((chunk, c_out, cols), bf16),
            dma((n,)),
            dma((n,)),
            dma,
            dma((chunk,)),
            dma((chunk, n)),
            dma((chunk, n)),
            dma,
            dma,
        ],
        compiler_params=pltpu.CompilerParams(
            collective_id=0, has_side_effects=True, vmem_limit_bytes=58 * 2**20),
        cost_estimate=pl.CostEstimate(flops=flops, bytes_accessed=4 * features.size * 2, transcendentals=features.size),
    )(
        features.reshape(n, chunk, ch, cols),
        mixing.reshape(3, n, chunk, cols),
        decay_rate.reshape(n, chunk, cols),
        gate_input.reshape(n, chunk, ch, cols),
        out_weight,
    )


def solution(mesh):
    n_rows, n = mesh.shape["rows"], mesh.shape["chan"]
    in_specs = (
        P("rows", "chan", None),
        P(None, "rows", None),
        P("rows", None),
        P("rows", "chan", None),
        P(),
    )
    out_specs = P(("rows", "chan"), None, None)
    return jax.shard_map(
        functools.partial(shards, n_rows, n), mesh=mesh, in_specs=in_specs, out_specs=out_specs, check_vma=False)
```

time: 317 us -> 182 us (0.57); the launches traced: 313 us -> 182 us
  Pallas kernels: 0 us -> 176 us
  blocking collectives: 142 us -> 0 us
  other arithmetic: 89.9 us -> 0 us
  matrix products: 39.7 us -> 0 us
  local copies, waits for them, and re-layouts: 23.2 us -> 5.89 us
  waiting for transfers between devices: 13.6 us -> 0 us
  starting transfers between devices: 3.88 us -> 0 us
    pallas_call x0 -> x1, Pallas kernels: none -> 176 us  [shards(): pl.pallas_call(functools.partial(kernel, n_rows, n), out_shape=jax.ShapeD...]
    all_to_all x1 -> x0, blocking collectives: 142 us -> none  [shards(): lax.all_to_all(mixed_in, 'chan', split_axis=0, concat_axis=1, tiled=True)]
    dynamic_update_slice x32 -> x0, other arithmetic: 70 us -> none  [shards(): lax.scan(advance, initial, (coef_steps, force_steps))]
    dot_general x17 -> x0, matrix products: 39.7 us -> none  [the longest x1 21.2 us: shards(): jnp.einsum('bcv,jbvw->jbcw', starts, ops_all, precision=highest)]
    ppermute x3 -> x0, waiting for transfers between devices: 13.6 us -> none  [from_behind(): return lax.ppermute(value, axis, pairs)]
    slice x48 -> x0, local copies, waits for them, and re-layouts: 10.3 us -> none  [the longest x32 10.1 us: spread(): before_col = jnp.concatenate([edge_col, current[..., :-1]], axis=-1)]
    mul x2 -> x0, other arithmetic: 9.22 us -> none  [the longest x1 9.2 us: shards(): forcing = in_scale[:, None, :] * features.astype(jnp.float32)]
    convert_element_type x2 -> x0, local copies, waits for them, and re-layouts: 8.73 us -> none  [the longest x1 8.6 us: shards(): return jnp.einsum('oc,rcw->row', out_weight, lax.all_to_all(mixed_in, 'ch...]
  transfers between devices with their start and end apart: 3 -> 0, of which waited for: 3 -> 0; matrix products, arithmetic and copies ran while one was open for 0% -> 0% of each run, Pallas kernels for 0% -> 0%
where the time goes in v1:
time: 182 us
  Pallas kernels  176 us (97%)
  local copies, waits for them, and re-layouts  5.89 us (3%)
    pallas_call x1, Pallas kernels, shards(): pl.pallas_call(functools.partial(kernel, n_rows, n), out_shape=jax.ShapeD...  176 us
    unnamed x1, local copies, waits for them, and re-layouts  5.89 us

profile of v1, /device:TPU:5, one launch (start us, length us, event | category | flops | bytes accessed | tf_op | source)
XLA Modules:
  0.0 182.0 jit_solution(16763305506649006447)
XLA Ops:
  0.0 176.1 %shard_map.55 = bf16[8,1536,256]{2,1,0:T(8,128)(2,1)} custom-call(bf16[8,8,192,256]{3,2,1,0:T(8,128)(2,1)} %bitcast.4, f32[3,8,8,256]{3,2,1,0:T(8,128)} %bitcast.6, f32[8,8,256]{2,1,0:T(8,128)} %bitcast.7, bf16[8,8,192,256]{3,2,1,0:T(8,128)(2,1)} %bitcast.5, bf16[1536,1536]{1,0:T(8,128)(2,1)} %w_hbm.1), custom_call_target="tpu_custom_call" | custom-call | flops 9663676416 | bytes 25165824 | tf_op jit(solution)/shard_map/pallas_call | solution.py:231
  176.1 5.9 %copy.7 = bf16[8,1536,256]{2,1,0:T(8,128)(2,1)} copy(bf16[8,1536,256]{2,1,0:T(8,128)(2,1)} %shard_map.55) | data formatting | bytes 12582912

commit v2 on v1

--- a/solution.py
+++ b/solution.py
@@ -8,11 +8,20 @@
 from jax.sharding import PartitionSpec as P
 
 MESH = pl.DeviceIdType.MESH
-HIGHEST = lax.Precision.HIGHEST
 
 
 def tile_of(size, choices):
     return next(t for t in choices if size % t == 0)
+
+
+def halves(value):
+    high = value.astype(jnp.bfloat16)
+    return high, (value - high.astype(jnp.float32)).astype(jnp.bfloat16)
+
+
+def dot3(a_hi, a_lo, b_hi, b_lo):
+    dot = functools.partial(jnp.dot, preferred_element_type=jnp.float32)
+    return dot(a_hi, b_hi) + (dot(a_hi, b_lo) + dot(a_lo, b_hi))
 
 
 def partner(me, k, n):
@@ -24,7 +33,8 @@
 
 
 def kernel(n_rows, n, feat_hbm, mix_ref, decay_ref, gate_hbm, w_hbm, out_hbm,
-           feat, gate, weight, coef, scale, band, ops, starts, tail, incoming, outgoing, sent, got, result,
+           feat, gate, weight, coef, scale, band, ops_hi, ops_lo, starts, tail,
+           incoming, outgoing, come_hi, come_lo, sent, got, result,
            feat_sem, gate_sem, weight_sem, out_sem, send_sem, recv_sem, relay_send, relay_recv):
     _, chunk, ch, cols = feat.shape
     c_out = weight.shape[0]
@@ -80,20 +90,23 @@
         push = scale[j, pl.ds(row, 1), :] * feat[j, row, at, :].astype(jnp.float32)
         return step(state, j, row) + push
 
+    def scan_tile(j, t):
+        at = pl.ds(t * tile, tile)
+        state = tail[at, :]
+        starts[j, at, :] = state
+        for row in range(chunk):
+            state = advance(state, j, row, at)
+        tail[at, :] = state
+
     tail[...] = jnp.zeros_like(tail)
 
-    @pl.loop(0, n)
-    def _(j):
-        feat_copy(j).wait()
-
-        @pl.loop(0, tiles)
-        def _(t):
-            at = pl.ds(pl.multiple_of(t * tile, tile), tile)
-            state = tail[at, :]
-            starts[j, at, :] = state
-            for row in range(chunk):
-                state = advance(state, j, row, at)
-            tail[at, :] = state
+    @pl.when(p == 0)
+    def _():
+        @pl.loop(0, n)
+        def _(j):
+            feat_copy(j).wait()
+            for t in range(tiles):
+                scan_tile(j, t)
 
     @pl.when(p > 0)
     def _():
@@ -108,38 +121,48 @@
         band[...] = value
         offset = (lax.broadcasted_iota(jnp.int32, (cols, cols), 0)
                   - lax.broadcasted_iota(jnp.int32, (cols, cols), 1))
-        ops[0] = jnp.where(offset == 0, 1.0, 0.0).astype(jnp.float32)
+        ops_hi[0] = jnp.where(offset == 0, 1.0, 0.0).astype(jnp.bfloat16)
+        ops_lo[0] = jnp.zeros((cols, cols), jnp.bfloat16)
 
         @pl.loop(0, n)
         def _(j):
+            feat_copy(j).wait()
             dense = jnp.zeros((cols, cols), jnp.float32)
             for k in range(2 * chunk + 1):
                 dense = jnp.where(offset == k - chunk, band[j, k:k + 1, :], dense)
-            ops[j + 1] = jnp.dot(ops[j], dense, precision=HIGHEST, preferred_element_type=jnp.float32)
+            product = dot3(ops_hi[j], ops_lo[j], *halves(dense))
+            ops_hi[j + 1], ops_lo[j + 1] = halves(product)
+            for t in range(tiles):
+                scan_tile(j, t)
 
     pl.semaphore_wait(barrier, n - 1 + jnp.where(p > 0, 1, 0) + jnp.where(p < n_rows - 1, 1, 0))
 
-    def relay(device):
+    def relay(device, t):
+        at = pl.ds(t * tile, tile)
         return pltpu.make_async_remote_copy(
-            src_ref=outgoing, dst_ref=incoming, send_sem=relay_send, recv_sem=relay_recv,
+            src_ref=outgoing.at[at, :], dst_ref=incoming.at[at, :],
+            send_sem=relay_send.at[t], recv_sem=relay_recv.at[t],
             device_id={"rows": device}, device_id_type=MESH)
 
-    @pl.when(p > 0)
-    def _():
-        relay(p - 1).wait_recv()
-
-    @pl.when(p < n_rows - 1)
-    def _():
-        @pl.when(p == 0)
-        def _():
-            outgoing[...] = tail[...]
+    for t in range(tiles):
+        at = pl.ds(t * tile, tile)
 
         @pl.when(p > 0)
         def _():
-            outgoing[...] = tail[...] + jnp.dot(
-                incoming[...], ops[n], precision=HIGHEST, preferred_element_type=jnp.float32)
-
-        relay(p + 1).start()
+            relay(p - 1, t).wait_recv()
+            come_hi[at, :], come_lo[at, :] = halves(incoming[at, :])
+
+        @pl.when(p < n_rows - 1)
+        def _():
+            @pl.when(p == 0)
+            def _():
+                outgoing[at, :] = tail[at, :]
+
+            @pl.when(p > 0)
+            def _():
+                outgoing[at, :] = tail[at, :] + dot3(come_hi[at, :], come_lo[at, :], ops_hi[n], ops_lo[n])
+
+            relay(p + 1, t).start()
 
     def send(row, k):
         return pltpu.make_async_remote_copy(
@@ -168,8 +191,7 @@
 
                 @pl.when(p > 0)
                 def _():
-                    starts[j] = starts[j] + jnp.dot(
-                        incoming[...], ops[j], precision=HIGHEST, preferred_element_type=jnp.float32)
+                    starts[j] = starts[j] + dot3(come_hi[...], come_lo[...], ops_hi[j], ops_lo[j])
 
             @pl.when(k < n - 1)
             def _():
@@ -215,20 +237,30 @@
 
     @pl.when(p < n_rows - 1)
     def _():
-        relay(p + 1).wait_send()
+        for t in range(tiles):
+            relay(p + 1, t).wait_send()
+
+
+def copy_kernel(source, target, sem):
+    copies = [pltpu.make_async_copy(source.at[i], target.at[i], sem.at[i]) for i in range(source.shape[0])]
+    for copy in copies:
+        copy.start()
+    for copy in copies:
+        copy.wait()
 
 
 def shards(n_rows, n, features, mixing, decay_rate, gate_input, out_weight):
     rows_here, ch, cols = features.shape
     chunk = rows_here // n
     c_out, c_in = out_weight.shape
+    tiles = ch // tile_of(ch, (64, 48, 32, 16))
     depth = -(-(2 * chunk + 1) // 8) * 8
     f32, bf16 = jnp.float32, jnp.bfloat16
     any_spec = pl.BlockSpec(memory_space=pl.ANY)
     vmem_spec = pl.BlockSpec(memory_space=pltpu.VMEM)
     dma = pltpu.SemaphoreType.DMA
     flops = 2 * chunk * c_out * c_in * cols
-    return pl.pallas_call(
+    projected = pl.pallas_call(
         functools.partial(kernel, n_rows, n),
         out_shape=jax.ShapeDtypeStruct((chunk, c_out, cols), bf16),
         in_specs=[any_spec, vmem_spec, vmem_spec, any_spec, any_spec],
@@ -240,11 +272,14 @@
             pltpu.VMEM((3, n, chunk, cols), f32),
             pltpu.VMEM((n, chunk, cols), f32),
             pltpu.VMEM((n, depth, cols), f32),
-            pltpu.VMEM((n + 1, cols, cols), f32),
+            pltpu.VMEM((n + 1, cols, cols), bf16),
+            pltpu.VMEM((n + 1, cols, cols), bf16),
             pltpu.VMEM((n, ch, cols), f32),
             pltpu.VMEM((ch, cols), f32),
             pltpu.VMEM((ch, cols), f32),
             pltpu.VMEM((ch, cols), f32),
+            pltpu.VMEM((ch, cols), bf16),
+            pltpu.VMEM((ch, cols), bf16),
             pltpu.VMEM((n, chunk, ch, cols), bf16),
             pltpu.VMEM((chunk, c_in, cols), bf16),
             pltpu.VMEM((chunk, c_out, cols), bf16),
@@ -254,8 +289,8 @@
             dma((chunk,)),
             dma((chunk, n)),
             dma((chunk, n)),
-            dma,
-            dma,
+            dma((tiles,)),
+            dma((tiles,)),
         ],
         compiler_params=pltpu.CompilerParams(
             collective_id=0, has_side_effects=True, vmem_limit_bytes=58 * 2**20),
@@ -267,6 +302,13 @@
         gate_input.reshape(n, chunk, ch, cols),
         out_weight,
     )
+    return pl.pallas_call(
+        copy_kernel,
+        out_shape=jax.ShapeDtypeStruct(projected.shape, bf16),
+        in_specs=[any_spec],
+        out_specs=any_spec,
+        scratch_shapes=[dma((chunk,))],
+    )(projected)
 
 
 def solution(mesh):

time: 182 us -> 359 us (1.97)
  Pallas kernels: 176 us -> 359 us
  local copies, waits for them, and re-layouts: 5.89 us -> 0 us
    pallas_call x0 -> x1, Pallas kernels: none -> 192 us  [shards(): pl.pallas_call(copy_kernel, out_shape=jax.ShapeDtypeStruct(projected.shap...]
    pallas_call x1, Pallas kernels: 176 us -> 168 us  [shards(): pl.pallas_call(functools.partial(kernel, n_rows, n), out_shape=jax.ShapeD...]
    unnamed x1 -> x0, local copies, waits for them, and re-layouts: 5.89 us -> none
where the time goes in v2:
time: 359 us
  Pallas kernels  359 us (100%)
    pallas_call x1, Pallas kernels, shards(): pl.pallas_call(copy_kernel, out_shape=jax.ShapeDtypeStruct(projected.shap...  192 us
    pallas_call x1, Pallas kernels, shards(): pl.pallas_call(functools.partial(kernel, n_rows, n), out_shape=jax.ShapeD...  168 us

profile of v2, /device:TPU:5, one launch (start us, length us, event | category | flops | bytes accessed | tf_op | source)
XLA Modules:
  0.0 359.3 jit_solution(11566812716781975210)
XLA Ops:
  0.0 167.6 %shard_map.55.source = bf16[8,1536,256]{2,1,0:T(8,128)(2,1)} custom-call(bf16[8,8,192,256]{3,2,1,0:T(8,128)(2,1)} %bitcast.4, f32[3,8,8,256]{3,2,1,0:T(8,128)} %bitcast.6, f32[8,8,256]{2,1,0:T(8,128)} %bitcast.7, bf16[8,8,192,256]{3,2,1,0:T(8,128)(2,1)} %bitcast.5, bf16[1536,1536]{1,0:T(8,128)(2,1)} %w_hbm.1), custom_call_target="tpu_custom_call" | custom-call | flops 9663676416 | bytes 25165824 | tf_op jit(solution)/shard_map/pallas_call | solution.py:263
  167.6 191.8 %shard_map.56 = bf16[8,1536,256]{2,1,0:T(8,128)(2,1)} custom-call(bf16[8,1536,256]{2,1,0:T(8,128)(2,1)} %shard_map.55.source), custom_call_target="tpu_custom_call" | custom-call | tf_op jit(solution)/shard_map/pallas_call | solution.py:305

commit v3 on v2

--- a/solution.py
+++ b/solution.py
@@ -26,10 +26,12 @@
 
 def partner(me, k, n):
     half = n // 2
-    side, place = me // half, me % half
-    across = (1 - side) * half + (place + k) % half
-    beside = side * half + (place + 1 + k - half) % half
-    return jnp.where(k < half, across, beside)
+    mask = jnp.where(k < half, n - 1 - k, (k - half + 1) % half)
+    result, bit = 0, 1
+    while bit < n:
+        result += (me // bit + mask // bit) % 2 * bit
+        bit *= 2
+    return result
 
 
 def kernel(n_rows, n, feat_hbm, mix_ref, decay_ref, gate_hbm, w_hbm, out_hbm,
@@ -241,11 +243,16 @@
             relay(p + 1, t).wait_send()
 
 
-def copy_kernel(source, target, sem):
-    copies = [pltpu.make_async_copy(source.at[i], target.at[i], sem.at[i]) for i in range(source.shape[0])]
-    for copy in copies:
+def copy_kernel(source, target, held, in_sem, out_sem):
+    rows = range(source.shape[0])
+    ins = [pltpu.make_async_copy(source.at[i], held.at[i], in_sem.at[i]) for i in rows]
+    outs = [pltpu.make_async_copy(held.at[i], target.at[i], out_sem.at[i]) for i in rows]
+    for copy in ins:
         copy.start()
-    for copy in copies:
+    for i in rows:
+        ins[i].wait()
+        outs[i].start()
+    for copy in outs:
         copy.wait()
 
 
@@ -307,7 +314,8 @@
         out_shape=jax.ShapeDtypeStruct(projected.shape, bf16),
         in_specs=[any_spec],
         out_specs=any_spec,
-        scratch_shapes=[dma((chunk,))],
+        scratch_shapes=[pltpu.VMEM(projected.shape, bf16), dma((chunk,)), dma((chunk,))],
+        compiler_params=pltpu.CompilerParams(vmem_limit_bytes=58 * 2**20),
     )(projected)
 
 

time: 359 us -> 171 us (0.48)
  Pallas kernels: 359 us -> 171 us
    pallas_call x1, Pallas kernels: 192 us -> 5.51 us  [shards(): pl.pallas_call(copy_kernel, out_shape=jax.ShapeDtypeStruct(projected.shap...]
where the time goes in v3:
time: 171 us
  Pallas kernels  171 us (100%)
    pallas_call x1, Pallas kernels, shards(): pl.pallas_call(functools.partial(kernel, n_rows, n), out_shape=jax.ShapeD...  165 us
    pallas_call x1, Pallas kernels, shards(): pl.pallas_call(copy_kernel, out_shape=jax.ShapeDtypeStruct(projected.shap...  5.51 us

profile of v3, /device:TPU:5, one launch (start us, length us, event | category | flops | bytes accessed | tf_op | source)
XLA Modules:
  0.0 170.6 jit_solution(13119055328008134713)
XLA Ops:
  0.0 165.1 %shard_map.55.source = bf16[8,1536,256]{2,1,0:T(8,128)(2,1)} custom-call(bf16[8,8,192,256]{3,2,1,0:T(8,128)(2,1)} %bitcast.4, f32[3,8,8,256]{3,2,1,0:T(8,128)} %bitcast.6, f32[8,8,256]{2,1,0:T(8,128)} %bitcast.7, bf16[8,8,192,256]{3,2,1,0:T(8,128)(2,1)} %bitcast.5, bf16[1536,1536]{1,0:T(8,128)(2,1)} %w_hbm.1), custom_call_target="tpu_custom_call" | custom-call | flops 9663676416 | bytes 25165824 | tf_op jit(solution)/shard_map/pallas_call | solution.py:270
  165.1 5.5 %shard_map.56 = bf16[8,1536,256]{2,1,0:T(8,128)(2,1)} custom-call(bf16[8,1536,256]{2,1,0:T(8,128)(2,1)} %shard_map.55.source), custom_call_target="tpu_custom_call" | custom-call | tf_op jit(solution)/shard_map/pallas_call | solution.py:312

commit v4 on v3

--- a/solution.py
+++ b/solution.py
@@ -181,8 +181,7 @@
             v = gate[j, row, at, :].astype(jnp.float32)
             put(t, (state * (v / (1.0 + jnp.exp(-v)))).astype(jnp.bfloat16))
 
-    @pl.loop(0, chunk)
-    def _(row):
+    def make_row(row):
         @pl.loop(0, n)
         def _(k):
             j = partner(me, k, n)
@@ -210,13 +209,10 @@
 
                 gated_row(j, row, put)
 
-    weight_copy.wait()
-
     def out_copy(row):
         return pltpu.make_async_copy(result.at[row], out_hbm.at[row], out_sem.at[row])
 
-    @pl.loop(0, chunk)
-    def _(row):
+    def project_row(row):
         @pl.loop(0, n - 1)
         def _(k):
             send(row, k).wait_recv()
@@ -229,12 +225,30 @@
 
         out_copy(row).start()
 
+    window = min(3, chunk)
+
+    @pl.loop(0, chunk + window)
+    def _(turn):
+        @pl.when(turn >= window)
+        def _():
+            @pl.loop(0, n - 1)
+            def _(k):
+                send(turn - window, k).wait_send()
+
+        @pl.when(turn < chunk)
+        def _():
+            make_row(turn)
+
+        @pl.when(turn == window)
+        def _():
+            weight_copy.wait()
+
+        @pl.when(turn >= window)
+        def _():
+            project_row(turn - window)
+
     @pl.loop(0, chunk)
     def _(row):
-        @pl.loop(0, n - 1)
-        def _(k):
-            send(row, k).wait_send()
-
         out_copy(row).wait()
 
     @pl.when(p < n_rows - 1)

time: 171 us -> 172 us (level)
  no operation moved by 1% of the time
where the time goes in v4:
time: 172 us
  Pallas kernels  172 us (100%)
    pallas_call x1, Pallas kernels, shards(): pl.pallas_call(functools.partial(kernel, n_rows, n), out_shape=jax.ShapeD...  166 us
    pallas_call x1, Pallas kernels, shards(): pl.pallas_call(copy_kernel, out_shape=jax.ShapeDtypeStruct(projected.shap...  5.51 us

profile of v4, /device:TPU:5, one launch (start us, length us, event | category | flops | bytes accessed | tf_op | source)
XLA Modules:
  0.0 171.7 jit_solution(3030127856360287077)
XLA Ops:
  0.0 166.2 %shard_map.55.source = bf16[8,1536,256]{2,1,0:T(8,128)(2,1)} custom-call(bf16[8,8,192,256]{3,2,1,0:T(8,128)(2,1)} %bitcast.4, f32[3,8,8,256]{3,2,1,0:T(8,128)} %bitcast.6, f32[8,8,256]{2,1,0:T(8,128)} %bitcast.7, bf16[8,8,192,256]{3,2,1,0:T(8,128)(2,1)} %bitcast.5, bf16[1536,1536]{1,0:T(8,128)(2,1)} %w_hbm.1), custom_call_target="tpu_custom_call" | custom-call | flops 9663676416 | bytes 25165824 | tf_op jit(solution)/shard_map/pallas_call | solution.py:284
  166.2 5.5 %shard_map.56 = bf16[8,1536,256]{2,1,0:T(8,128)(2,1)} custom-call(bf16[8,1536,256]{2,1,0:T(8,128)(2,1)} %shard_map.55.source), custom_call_target="tpu_custom_call" | custom-call | tf_op jit(solution)/shard_map/pallas_call | solution.py:326

commit v5 on v3

--- a/solution.py
+++ b/solution.py
@@ -34,10 +34,10 @@
     return result
 
 
-def kernel(n_rows, n, feat_hbm, mix_ref, decay_ref, gate_hbm, w_hbm, out_hbm,
-           feat, gate, weight, coef, scale, band, ops_hi, ops_lo, starts, tail,
+def kernel(n_rows, n, feat_hbm, mix_hbm, decay_hbm, gate_hbm, w_hbm, out_hbm,
+           feat, gate, mix, decay, weight, coef, scale, band, ops_hi, ops_lo, starts, tail,
            incoming, outgoing, come_hi, come_lo, sent, got, result,
-           feat_sem, gate_sem, weight_sem, out_sem, send_sem, recv_sem, relay_send, relay_recv):
+           feat_sem, gate_sem, mix_sem, decay_sem, weight_sem, out_sem, send_sem, recv_sem, relay_send, relay_recv):
     _, chunk, ch, cols = feat.shape
     c_out = weight.shape[0]
     p, me = lax.axis_index("rows"), lax.axis_index("chan")
@@ -53,16 +53,15 @@
 
     weight_copy = pltpu.make_async_copy(w_hbm, weight, weight_sem)
 
+    mix_copy = pltpu.make_async_copy(mix_hbm, mix, mix_sem)
+    decay_copy = pltpu.make_async_copy(decay_hbm, decay, decay_sem)
+    mix_copy.start()
+    decay_copy.start()
+
     @pl.loop(0, n)
     def _(j):
         feat_copy(j).start()
 
-    @pl.loop(0, n)
-    def _(j):
-        gate_copy(j).start()
-
-    weight_copy.start()
-
     barrier = pltpu.get_barrier_semaphore()
 
     @pl.loop(0, n - 1)
@@ -77,10 +76,12 @@
     def _():
         pl.semaphore_signal(barrier, inc=1, device_id={"rows": p + 1}, device_id_type=MESH)
 
-    retain = 1.0 - decay_ref[...]
+    mix_copy.wait()
+    decay_copy.wait()
+    retain = 1.0 - decay[...]
     for s in range(3):
-        coef[s] = retain * mix_ref[s]
-    scale[...] = jnp.sqrt(decay_ref[...])
+        coef[s] = retain * mix[s]
+    scale[...] = jnp.sqrt(decay[...])
 
     def step(state, j, row):
         left_w = coef[0, j, pl.ds(row, 1), :]
@@ -107,6 +108,7 @@
         @pl.loop(0, n)
         def _(j):
             feat_copy(j).wait()
+            gate_copy(partner(me, j, n)).start()
             for t in range(tiles):
                 scan_tile(j, t)
 
@@ -123,20 +125,36 @@
         band[...] = value
         offset = (lax.broadcasted_iota(jnp.int32, (cols, cols), 0)
                   - lax.broadcasted_iota(jnp.int32, (cols, cols), 1))
+        half, edge = cols // 2, -(-chunk // 8) * 8
+
+        def block(j, top, height, left):
+            block_offset = offset[top:top + height, left:left + half]
+            value = jnp.zeros((height, half), jnp.float32)
+            for k in range(2 * chunk + 1):
+                value = jnp.where(block_offset == k - chunk, band[j, k:k + 1, left:left + half], value)
+            return value
+
+        def dense_of(j):
+            empty = jnp.zeros((half - edge, half), jnp.float32)
+            upper = jnp.concatenate([empty, block(j, half - edge, edge, half)], axis=0)
+            lower = jnp.concatenate([block(j, half, edge, 0), empty], axis=0)
+            return jnp.concatenate([
+                jnp.concatenate([block(j, 0, half, 0), upper], axis=1),
+                jnp.concatenate([lower, block(j, half, half, half)], axis=1)], axis=0)
+
         ops_hi[0] = jnp.where(offset == 0, 1.0, 0.0).astype(jnp.bfloat16)
         ops_lo[0] = jnp.zeros((cols, cols), jnp.bfloat16)
 
         @pl.loop(0, n)
         def _(j):
             feat_copy(j).wait()
-            dense = jnp.zeros((cols, cols), jnp.float32)
-            for k in range(2 * chunk + 1):
-                dense = jnp.where(offset == k - chunk, band[j, k:k + 1, :], dense)
-            product = dot3(ops_hi[j], ops_lo[j], *halves(dense))
+            gate_copy(partner(me, j, n)).start()
+            product = dot3(ops_hi[j], ops_lo[j], *halves(dense_of(j)))
             ops_hi[j + 1], ops_lo[j + 1] = halves(product)
             for t in range(tiles):
                 scan_tile(j, t)
 
+    weight_copy.start()
     pl.semaphore_wait(barrier, n - 1 + jnp.where(p > 0, 1, 0) + jnp.where(p < n_rows - 1, 1, 0))
 
     def relay(device, t):
@@ -264,17 +282,18 @@
     depth = -(-(2 * chunk + 1) // 8) * 8
     f32, bf16 = jnp.float32, jnp.bfloat16
     any_spec = pl.BlockSpec(memory_space=pl.ANY)
-    vmem_spec = pl.BlockSpec(memory_space=pltpu.VMEM)
     dma = pltpu.SemaphoreType.DMA
     flops = 2 * chunk * c_out * c_in * cols
     projected = pl.pallas_call(
         functools.partial(kernel, n_rows, n),
         out_shape=jax.ShapeDtypeStruct((chunk, c_out, cols), bf16),
-        in_specs=[any_spec, vmem_spec, vmem_spec, any_spec, any_spec],
+        in_specs=[any_spec] * 5,
         out_specs=any_spec,
         scratch_shapes=[
             pltpu.VMEM((n, chunk, ch, cols), bf16),
             pltpu.VMEM((n, chunk, ch, cols), bf16),
+            pltpu.VMEM((3, n, chunk, cols), f32),
+            pltpu.VMEM((n, chunk, cols), f32),
             pltpu.VMEM((c_out, c_in), bf16),
             pltpu.VMEM((3, n, chunk, cols), f32),
             pltpu.VMEM((n, chunk, cols), f32),
@@ -292,6 +311,8 @@
             pltpu.VMEM((chunk, c_out, cols), bf16),
             dma((n,)),
             dma((n,)),
+            dma,
+            dma,
             dma,
             dma((chunk,)),
             dma((chunk, n)),

time: 171 us -> 170 us (level)
  no operation moved by 1% of the time
where the time goes in v5:
time: 170 us
  Pallas kernels  170 us (100%)
    pallas_call x1, Pallas kernels, shards(): pl.pallas_call(functools.partial(kernel, n_rows, n), out_shape=jax.ShapeD...  164 us
    pallas_call x1, Pallas kernels, shards(): pl.pallas_call(copy_kernel, out_shape=jax.ShapeDtypeStruct(projected.shap...  5.51 us

profile of v5, /device:TPU:5, one launch (start us, length us, event | category | flops | bytes accessed | tf_op | source)
XLA Modules:
  0.0 169.9 jit_solution(16759577302144375346)
XLA Ops:
  0.0 164.4 %shard_map.55.source = bf16[8,1536,256]{2,1,0:T(8,128)(2,1)} custom-call(bf16[8,8,192,256]{3,2,1,0:T(8,128)(2,1)} %bitcast.4, f32[3,8,8,256]{3,2,1,0:T(8,128)} %bitcast.6, f32[8,8,256]{2,1,0:T(8,128)} %bitcast.7, bf16[8,8,192,256]{3,2,1,0:T(8,128)(2,1)} %bitcast.5, bf16[1536,1536]{1,0:T(8,128)(2,1)} %w_hbm.1), custom_call_target="tpu_custom_call" | custom-call | flops 9663676416 | bytes 25165824 | tf_op jit(solution)/shard_map/pallas_call | solution.py:287
  164.4 5.5 %shard_map.56 = bf16[8,1536,256]{2,1,0:T(8,128)(2,1)} custom-call(bf16[8,1536,256]{2,1,0:T(8,128)(2,1)} %shard_map.55.source), custom_call_target="tpu_custom_call" | custom-call | tf_op jit(solution)/shard_map/pallas_call | solution.py:333

commit v6 on v5

--- a/solution.py
+++ b/solution.py
@@ -202,7 +202,8 @@
     @pl.loop(0, chunk)
     def _(row):
         @pl.loop(0, n)
-        def _(k):
+        def _(turn):
+            k = jnp.where((row == chunk - 1) & (turn < n - 1), (turn + n // 2) % (n - 1), turn)
             j = partner(me, k, n)
 
             @pl.when(row == 0)
@@ -265,11 +266,13 @@
     rows = range(source.shape[0])
     ins = [pltpu.make_async_copy(source.at[i], held.at[i], in_sem.at[i]) for i in rows]
     outs = [pltpu.make_async_copy(held.at[i], target.at[i], out_sem.at[i]) for i in rows]
-    for copy in ins:
+    for copy in ins[:3]:
         copy.start()
     for i in rows:
         ins[i].wait()
         outs[i].start()
+        for copy in ins[i + 3:i + 4]:
+            copy.start()
     for copy in outs:
         copy.wait()
 

time: 170 us -> 171 us (level)
  no operation moved by 1% of the time
where the time goes in v6:
time: 171 us
  Pallas kernels  171 us (100%)
    pallas_call x1, Pallas kernels, shards(): pl.pallas_call(functools.partial(kernel, n_rows, n), out_shape=jax.ShapeD...  164 us
    pallas_call x1, Pallas kernels, shards(): pl.pallas_call(copy_kernel, out_shape=jax.ShapeDtypeStruct(projected.shap...  6.22 us

profile of v6, /device:TPU:5, one launch (start us, length us, event | category | flops | bytes accessed | tf_op | source)
XLA Modules:
  0.0 170.7 jit_solution(2441461875400334058)
XLA Ops:
  0.0 164.4 %shard_map.55.source = bf16[8,1536,256]{2,1,0:T(8,128)(2,1)} custom-call(bf16[8,8,192,256]{3,2,1,0:T(8,128)(2,1)} %bitcast.4, f32[3,8,8,256]{3,2,1,0:T(8,128)} %bitcast.6, f32[8,8,256]{2,1,0:T(8,128)} %bitcast.7, bf16[8,8,192,256]{3,2,1,0:T(8,128)(2,1)} %bitcast.5, bf16[1536,1536]{1,0:T(8,128)(2,1)} %w_hbm.1), custom_call_target="tpu_custom_call" | custom-call | flops 9663676416 | bytes 25165824 | tf_op jit(solution)/shard_map/pallas_call | solution.py:290
  164.4 6.2 %shard_map.56 = bf16[8,1536,256]{2,1,0:T(8,128)(2,1)} custom-call(bf16[8,1536,256]{2,1,0:T(8,128)(2,1)} %shard_map.55.source), custom_call_target="tpu_custom_call" | custom-call | tf_op jit(solution)/shard_map/pallas_call | solution.py:336
